TPU v7x, 32 devices: a whole 2x2x4 slice. The times are simulated.
32 devices in a mesh: expert: 8 (over y, x, core), dp: 4 (over z).
Axes of the slice: x: 2, y: 2, z: 4, core: 2. Of those that a mesh axis runs over, the one named last changes fastest.
Arguments:
- tokens: bfloat16 [4096, 2048], P(('expert', 'dp')), may hold values from -6 to 6
- expert_ids: int32 [4096, 8], P(('expert', 'dp')), may hold values from 0 to 63, all different within a row; in each aligned block of 128 rows (0 to 127, 128 to 255, ...) at most 20 rows name the same one
- gate_probs: float32 [4096, 8], P(('expert', 'dp')), may hold values from 0.02 to 0.4
- cotangent: bfloat16 [4096, 2048], P(('expert', 'dp')), may hold values from -6 to 6
- weight_in: bfloat16 [64, 2048, 768], P('expert'), may hold values from -0.125 to 0.125
- weight_down: bfloat16 [64, 384, 2048], P('expert'), may hold values from -0.3125 to 0.3125
- swap_flag: int32 [8], replicated, may hold values from 0 to 1, as said below
Outputs:
- layer_out: bfloat16 [4096, 2048], P(('expert', 'dp'))
- gate_grads: float32 [4096, 8], P(('expert', 'dp'))
- token_grads: bfloat16 [4096, 2048], P(('expert', 'dp'))
- grad_in: float32 [64, 2048, 768], P('expert', 'dp')
- grad_down: float32 [64, 384, 2048], P('expert', None, 'dp')
Inputs may be any that keep to these rules, and one draw needn't show every extreme that they name: `expert_ids`: each row names 8 different experts. Among the 128 rows of one device no expert is named more than 20 times, and in some of these aligned blocks an expert is named exactly 20 times. swap_flag[i] = swap_flag[i XOR 2]. Where swap_flag[i] is 1, index i of the expert axis takes over the 8 experts of index i XOR 2; experts j * 8 to (j + 1) * 8 - 1 start on index j.
All inputs are finite; a program needn't handle non-finite values.
Results may differ from a plain program's by a relative error of at most 0.0085.
Values may be sent and summed in bfloat16 or wider, within the bound.
A program may use at most 192 MiB of HBM per device.

v0:
```python
import jax
import jax.numpy as jnp
from jax import lax
from jax.sharding import PartitionSpec as P

FF = 384
EXPERTS = 64
TOP = 8
CAP = 20


def swapped(block, axis, apart):
    count = lax.axis_size(axis)
    route = []
    for low in range(count):
        high = low | 1 << apart
        if high != low and high < count:
            route += [(low, high), (high, low)]
    return lax.ppermute(block, axis, route)


def body(tokens, expert_ids, gate_probs, cotangent, weight_in, weight_down, swap_flag):
    row_count = tokens.shape[0]
    model_width = tokens.shape[1]
    per_device = weight_in.shape[0]
    groups = lax.axis_size("expert")
    device_ids = jnp.arange(groups, dtype=jnp.int32)
    my_index = lax.axis_index("expert")
    my_flag = jnp.sum(jnp.where(device_ids == my_index, swap_flag, 0))
    expert_range = jnp.arange(EXPERTS, dtype=jnp.int32)
    home_device = expert_range // per_device
    moved_flag = jnp.sum(
        jnp.where(home_device[:, None] == device_ids[None, :], swap_flag[None, :], 0), axis=1
    )
    target_device = jnp.bitwise_xor(home_device, 2 * moved_flag)
    partner_in, partner_down = swapped((weight_in, weight_down), "expert", 1)
    use_in = jnp.where(my_flag == 1, partner_in, weight_in)
    use_down = jnp.where(my_flag == 1, partner_down, weight_down)
    dest_place = target_device * per_device + expert_range % per_device
    flat_ids = expert_ids.reshape(-1)
    onehot = (flat_ids[:, None] == expert_range[None, :]).astype(jnp.int32)
    slot_rank = jnp.sum((jnp.cumsum(onehot, axis=0) - onehot) * onehot, axis=1)
    place_of = jnp.sum(onehot * dest_place[None, :], axis=1)
    slot_index = place_of * CAP + slot_rank
    token_copies = jnp.repeat(tokens, TOP, axis=0)
    grad_rows = (gate_probs[:, :, None] * cotangent[:, None, :].astype(jnp.float32)).astype(
        jnp.bfloat16
    )
    grad_rows = grad_rows.reshape(row_count * TOP, model_width)
    empty_rows = jnp.zeros((EXPERTS * CAP, model_width), jnp.bfloat16)
    send_x = (
        empty_rows.at[slot_index].set(token_copies).reshape(groups, per_device, CAP, model_width)
    )
    send_grad = (
        empty_rows.at[slot_index].set(grad_rows).reshape(groups, per_device, CAP, model_width)
    )
    recv_x, recv_grad = (
        lax.all_to_all(send_x, "expert", split_axis=0, concat_axis=0, tiled=True),
        lax.all_to_all(send_grad, "expert", split_axis=0, concat_axis=0, tiled=True),
    )
    projected = jnp.einsum("nscd,sdf->nscf", recv_x, use_in, preferred_element_type=jnp.float32)
    pre_gate = projected[..., :FF]
    up_part = projected[..., FF:]
    sigmoid_gate = jax.nn.sigmoid(pre_gate)
    activated = pre_gate * sigmoid_gate
    hidden = (activated * up_part).astype(jnp.bfloat16)
    expert_out = jnp.einsum(
        "nscf,sfd->nscd", hidden, use_down, preferred_element_type=jnp.float32
    ).astype(jnp.bfloat16)
    hidden_grad = jnp.einsum(
        "nscd,sfd->nscf", recv_grad, use_down, preferred_element_type=jnp.float32
    )
    gate_grad = hidden_grad * up_part * sigmoid_gate * (1.0 + pre_gate * (1.0 - sigmoid_gate))
    proj_grad = jnp.concatenate([gate_grad, hidden_grad * activated], axis=-1).astype(jnp.bfloat16)
    row_grad = jnp.einsum(
        "nscf,sdf->nscd", proj_grad, use_in, preferred_element_type=jnp.float32
    ).astype(jnp.bfloat16)
    home_out, home_grad = (
        lax.all_to_all(expert_out, "expert", split_axis=0, concat_axis=0, tiled=True),
        lax.all_to_all(row_grad, "expert", split_axis=0, concat_axis=0, tiled=True),
    )
    grad_first = jnp.einsum("nscd,nscf->sdf", recv_x, proj_grad, preferred_element_type=jnp.float32)
    grad_second = jnp.einsum(
        "nscf,nscd->sfd", hidden, recv_grad, preferred_element_type=jnp.float32
    )
    reduced_in, reduced_down = (
        lax.psum_scatter(
            grad_first.astype(jnp.bfloat16), "dp", scatter_dimension=1, tiled=True
        ).astype(jnp.float32),
        lax.psum_scatter(
            grad_second.astype(jnp.bfloat16), "dp", scatter_dimension=2, tiled=True
        ).astype(jnp.float32),
    )
    out_rows = home_out.reshape(EXPERTS * CAP, model_width)[slot_index]
    out_rows = out_rows.astype(jnp.float32).reshape(row_count, TOP, model_width)
    layer_out = jnp.sum(gate_probs[:, :, None] * out_rows, axis=1).astype(jnp.bfloat16)
    gate_grads = jnp.sum(cotangent[:, None, :].astype(jnp.float32) * out_rows, axis=2)
    back_rows = home_grad.reshape(EXPERTS * CAP, model_width)[slot_index]
    back_rows = back_rows.astype(jnp.float32).reshape(row_count, TOP, model_width)
    token_grads = jnp.sum(back_rows, axis=1).astype(jnp.bfloat16)
    return (layer_out, gate_grads, token_grads, reduced_in, reduced_down)


def solution(mesh):
    in_specs = (
        P(("expert", "dp"), None),
        P(("expert", "dp"), None),
        P(("expert", "dp"), None),
        P(("expert", "dp"), None),
        P("expert", None, None),
        P("expert", None, None),
        P(),
    )
    out_specs = (
        P(("expert", "dp"), None),
        P(("expert", "dp"), None),
        P(("expert", "dp"), None),
        P("expert", "dp", None),
        P("expert", None, "dp"),
    )
    return jax.shard_map(body, mesh=mesh, in_specs=in_specs, out_specs=out_specs, check_vma=False)
```

profile of v0, /device:TPU:0, one launch (start us, length us, event | category | flops | bytes accessed | tf_op | source)
XLA Modules:
  0.0 1613.0 jit_solution(9995312774237912552)
XLA Ops:
  11.2 18.0 %reduce-window.6 = s32[64,8,128]{2,1,0:T(8,128)S(1)} reduce-window(s32[64,8,128]{2,1,0:T(8,128)S(1)} %fusion.41, s32[]{:T(128)} %constant.49.clone.1), window={size=1x1x128 pad=0_0x0_0x127_0}, to_apply=%region_3.4 | reduce-window | flops 8323072 | bytes 524292 | tf_op jit(solution)/shard_map/reduce-window
  30.7 9.7 scatter_custom_fusion
  40.3 8.9 reshape.132
  49.2 8.5 copy.45
  57.8 5.0 all-to-all-start
  65.1 10.0 scatter_custom_fusion.1
  75.1 8.9 reshape.134
  84.0 8.5 copy.50
  93.8 515.2 %all-to-all-done = bf16[8,8,20,2048]{3,1,2,0:T(8,128)(2,1)} async-done(((bf16[8,8,20,2048]{3,1,2,0:T(8,128)(2,1)}), bf16[8,8,20,2048]{3,1,2,0:T(8,128)(2,1)}, u32[]{:S(2)}, u32[]{:S(2)}) %all-to-all-start) | async-done | bytes 5242912 | tf_op jit(solution)/shard_map/all_to_all | solution.py:58
  613.9 15.8 fusion.32
  629.7 304.0 %all-to-all-done.2 = bf16[8,8,20,2048]{3,1,2,0:T(8,128)(2,1)} async-done(((bf16[8,8,20,2048]{3,1,2,0:T(8,128)(2,1)}), bf16[8,8,20,2048]{3,1,2,0:T(8,128)(2,1)}, u32[]{:S(2)}, u32[]{:S(2)}) %all-to-all-start.2) | async-done | bytes 5242912 | tf_op jit(solution)/shard_map/all_to_all | solution.py:59
  933.7 18.0 %fusion.29 = (bf16[8,8,20,384]{3,2,0,1:T(8,128)(2,1)S(1)}, bf16[8,8,20,384]{3,2,0,1:T(8,128)(2,1)S(1)}, bf16[8,8,20,384]{3,2,0,1:T(8,128)(2,1)}) fusion(f32[8,8,20,768]{3,2,0,1:T(8,128)} %fusion.32, bf16[8,8,20,2048]{3,1,2,0:T(8,128)(2,1)} %all-to-all-done.2, bf16[8,384,2048]{2,1,0:T(8,128)(2,1)} %collective-permute-done, bf16[8,384,2048]{2,1,0:T(8,128)(2,1)} %param.12, ...), kind=kOutput, calls=%fused_computation.41 | convolution fusion | flops 2026930176 | bytes 37289984 | tf_op jit(solution)/shard_map/nscd,sfd->nscf/dot_general | solution.py:70
  951.7 15.2 bitcast_convert_fusion.1
  966.9 34.0 %bitcast_convert_fusion = bf16[8,2048,768]{2,1,0:T(8,128)(2,1)} fusion(bf16[8,8,20,2048]{3,1,2,0:T(8,128)(2,1)} %all-to-all-done, bf16[8,8,20,384]{3,2,0,1:T(8,128)(2,1)S(1)} %get-tuple-element.20, bf16[8,8,20,384]{3,2,0,1:T(8,128)(2,1)S(1)} %get-tuple-element.19), kind=kOutput, calls=%fused_computation.4 | convolution fusion | flops 4043046912 | bytes 32374784 | tf_op jit(solution)/shard_map/nscd,nscf->sdf/dot_general | solution.py:82
  1000.9 9.0 convert_bitcast_fusion.1
  1009.9 8.5 copy.47
  1023.1 18.1 %convert_bitcast_fusion = bf16[8,8,20,2048]{3,2,0,1:T(8,128)(2,1)} fusion(bf16[8,2048,768]{2,1,0:T(8,128)(2,1)} %collective-permute-done.1, bf16[8,2048,768]{2,1,0:T(8,128)(2,1)} %param.11, pred[]{:T(512)S(6)} %eq.52, bf16[8,8,20,384]{3,2,0,1:T(8,128)(2,1)S(1)} %get-tuple-element.20, bf16[8,8,20,384]{3,2,0,1:T(8,128)(2,1)S(1)} %get-tuple-element.19), kind=kOutput, calls=%fused_computation.22 | convolution fusion | flops 4045668352 | bytes 57540608 | tf_op jit(solution)/shard_map/nscf,sdf->nscd/dot_general | solution.py:75
  1041.2 8.6 copy.52
  1049.8 33.6 %all-to-all-done.1 = bf16[8,8,20,2048]{3,1,2,0:T(8,128)(2,1)} async-done(((bf16[8,8,20,2048]{3,1,2,0:T(8,128)(2,1)}), bf16[8,8,20,2048]{3,1,2,0:T(8,128)(2,1)}, u32[]{:S(2)}, u32[]{:S(2)}) %all-to-all-start.1) | async-done | bytes 5242912 | tf_op jit(solution)/shard_map/all_to_all | solution.py:79
  1083.4 4.9 all-to-all-start.3
  1088.3 8.8 copy.48
  1097.1 9.0 reshape.133
  1106.1 12.1 gather_fusion
  1118.2 5.7 fusion.9
  1124.5 24.1 %all-to-all-done.3 = bf16[8,8,20,2048]{3,1,2,0:T(8,128)(2,1)} async-done(((bf16[8,8,20,2048]{3,1,2,0:T(8,128)(2,1)}), bf16[8,8,20,2048]{3,1,2,0:T(8,128)(2,1)}, u32[]{:S(2)}, u32[]{:S(2)}) %all-to-all-start.3) | async-done | bytes 5242912 | tf_op jit(solution)/shard_map/all_to_all | solution.py:80
  1148.7 8.8 copy.53
  1157.4 9.0 reshape.135
  1166.5 12.2 gather_fusion.1
  1178.7 5.9 bitcast_reduce_fusion
  1184.6 6.1 convert_element_type.76
  1190.7 406.3 %reduce-scatter.3.cloned.1.call-done = bf16[8,512,768]{2,1,0:T(8,128)(2,1)} async-done(((bf16[8,2048,768]{2,1,0:T(8,128)(2,1)}), bf16[8,512,768]{2,1,0:T(8,128)(2,1)}) %reduce-scatter.3.cloned.1.call-update) | async-done | bytes 6291472 | tf_op jit(solution)/shard_map/reduce_scatter | solution.py:87
  1597.0 8.7 convert_element_type.74
  (55 shorter events, 18.7 us)
Async XLA Ops:
  7.2 23.5 %copy-start = (bf16[128,2048]{1,0:T(8,128)(2,1)S(1)}, bf16[128,2048]{1,0:T(8,128)(2,1)}, u32[]{:S(2)}) copy-start(bf16[128,2048]{1,0:T(8,128)(2,1)} %param.7) | copy-start | bytes 1572868
  7.2 606.7 %collective-permute-start.1 = (bf16[8,2048,768]{2,1,0:T(8,128)(2,1)}, bf16[8,2048,768]{2,1,0:T(8,128)(2,1)}, u32[]{:S(2)}, u32[]{:S(2)}) collective-permute-start(bf16[8,2048,768]{2,1,0:T(8,128)(2,1)} %param.11), channel_id=1, source_target_pairs={{0,8},{8,0},{4,12},{12,4},{16,24},{24,16},{20,28},{28,20},{1,9},{9... | collective-permute-start | bytes 75497480 | tf_op jit(solution)/shard_map/ppermute | solution.py:19
  30.6 34.4 %copy-start.7 = (s32[1024,1]{0,1:T(1,128)}, s32[1024,1]{0,1:T(1,128)S(1)}, u32[]{:S(2)}) copy-start(s32[1024,1]{0,1:T(1,128)S(1)} %compare_select_fusion) | copy-start | bytes 12292
  57.7 7.0 copy-start.9
  57.8 7.2 copy-start.6
  57.8 551.3 %all-to-all-start = ((bf16[8,8,20,2048]{3,1,2,0:T(8,128)(2,1)}), bf16[8,8,20,2048]{3,1,2,0:T(8,128)(2,1)}, u32[]{:S(2)}, u32[]{:S(2)}) async-start(bf16[8,8,20,2048]{3,1,2,0:T(8,128)(2,1)} %copy.45), calls=%async_computation | async-start | bytes 10485760 | tf_op jit(solution)/shard_map/all_to_all | solution.py:58
  62.7 871.0 %collective-permute-start = (bf16[8,384,2048]{2,1,0:T(8,128)(2,1)}, bf16[8,384,2048]{2,1,0:T(8,128)(2,1)}, u32[]{:S(2)}, u32[]{:S(2)}) collective-permute-start(bf16[8,384,2048]{2,1,0:T(8,128)(2,1)} %param.12), channel_id=1, source_target_pairs={{0,8},{8,0},{4,12},{12,4},{16,24},{24,16},{20,28},{28,20},{1,9},{9... | collective-permute-start | bytes 37748744 | tf_op jit(solution)/shard_map/ppermute | solution.py:19
  64.9 19.2 %copy-start.4 = (f32[128,8]{1,0:T(8,128)}, f32[128,8]{1,0:T(8,128)S(1)}, u32[]{:S(2)}) copy-start(f32[128,8]{1,0:T(8,128)S(1)} %copy.40) | copy-start | bytes 12292
  65.1 18.9 %copy-start.2 = (f32[128,2048]{1,0:T(8,128)}, f32[128,2048]{1,0:T(8,128)S(1)}, u32[]{:S(2)}) copy-start(f32[128,2048]{1,0:T(8,128)S(1)} %convert_element_type.69) | copy-start | bytes 3145732
  84.0 8.5 copy-start.10
  609.0 324.7 %all-to-all-start.2 = ((bf16[8,8,20,2048]{3,1,2,0:T(8,128)(2,1)}), bf16[8,8,20,2048]{3,1,2,0:T(8,128)(2,1)}, u32[]{:S(2)}, u32[]{:S(2)}) async-start(bf16[8,8,20,2048]{3,1,2,0:T(8,128)(2,1)} %copy.50), calls=%async_computation.2 | async-start | bytes 10485760 | tf_op jit(solution)/shard_map/all_to_all | solution.py:59
  613.7 570.9 %reduce-scatter.5.cloned.1.call-start = ((), (), s32[]{:S(2)}) async-start(), calls=%async_computation.7 | async-start | bytes 15728640 | tf_op jit(solution)/shard_map/reduce_scatter | solution.py:90
  966.9 630.2 %reduce-scatter.3.cloned.1.call-start = ((), (), s32[]{:S(2)}) async-start(), calls=%async_computation.6 | async-start | bytes 31457280 | tf_op jit(solution)/shard_map/reduce_scatter | solution.py:87
  1018.4 65.0 %all-to-all-start.1 = ((bf16[8,8,20,2048]{3,1,2,0:T(8,128)(2,1)}), bf16[8,8,20,2048]{3,1,2,0:T(8,128)(2,1)}, u32[]{:S(2)}, u32[]{:S(2)}) async-start(bf16[8,8,20,2048]{3,1,2,0:T(8,128)(2,1)} %copy.47), calls=%async_computation.1 | async-start | bytes 10485760 | tf_op jit(solution)/shard_map/all_to_all | solution.py:79
  1049.8 38.5 %copy-start.8 = (s32[1024,1]{0,1:T(1,128)S(1)}, s32[1024,1]{0,1:T(1,128)}, u32[]{:S(2)}) copy-start(s32[1024,1]{0,1:T(1,128)} %copy-done.7) | copy-start | bytes 12292
  1083.4 65.2 %all-to-all-start.3 = ((bf16[8,8,20,2048]{3,1,2,0:T(8,128)(2,1)}), bf16[8,8,20,2048]{3,1,2,0:T(8,128)(2,1)}, u32[]{:S(2)}, u32[]{:S(2)}) async-start(bf16[8,8,20,2048]{3,1,2,0:T(8,128)(2,1)} %copy.52), calls=%async_computation.3 | async-start | bytes 10485760 | tf_op jit(solution)/shard_map/all_to_all | solution.py:80
  1106.1 12.1 copy-start.3
  1106.1 12.1 copy-start.5
  1184.6 421.1 %copy-start.1 = (bf16[128,2048]{1,0:T(8,128)(2,1)S(1)}, bf16[128,2048]{1,0:T(8,128)(2,1)}, u32[]{:S(2)}) copy-start(bf16[128,2048]{1,0:T(8,128)(2,1)} %param.7) | copy-start | bytes 1572868
Sparse Core Ops, SparseCore 0:
  967.0 212.1 reduce-scatter.4
  1181.5 415.4 reduce-scatter.2
where the time goes:
time: 1620 us; the launch traced here: 1610 us
  waiting for transfers between devices  1280 us (79%)
  local copies, waits for them, and re-layouts  124 us (8%)
  matrix products  110 us (7%)
  other arithmetic  56.2 us (3%)
  starting transfers between devices  24.4 us (2%)
    all_to_all x1, waiting for transfers between devices, body(): lax.all_to_all(send_x, 'expert', split_axis=0, concat_axis=0, tiled=True)  515 us
    reduce_scatter x1, waiting for transfers between devices, body(): lax.psum_scatter(grad_first.astype(jnp.bfloat16), 'dp', scatter_dimension...  406 us
    all_to_all x1, waiting for transfers between devices, body(): lax.all_to_all(send_grad, 'expert', split_axis=0, concat_axis=0, tiled=True)  304 us
    dot_general x1, matrix products, body(): jnp.einsum('nscd,nscf->sdf', recv_x, proj_grad, preferred_element_type=jn...  34 us
    all_to_all x1, waiting for transfers between devices, body(): lax.all_to_all(expert_out, 'expert', split_axis=0, concat_axis=0, tiled=T...  33.6 us
  transfers between devices with their start and end apart: 8, of which 5 were waited for; matrix products, arithmetic and copies ran while one was open for 15% of the time, Pallas kernels for 0%

commit v1 on v0

v1 whole, which is shorter than its diff:
```python
import jax
import jax.numpy as jnp
from jax import lax
from jax.sharding import PartitionSpec as P

FF = 384
EXPERTS = 64
TOP = 8
CAP = 20


def swapped(block, axis, apart):
    count = lax.axis_size(axis)
    route = []
    for low in range(count):
        high = low | 1 << apart
        if high != low and high < count:
            route += [(low, high), (high, low)]
    return lax.ppermute(block, axis, route)


def body(tokens, expert_ids, gate_probs, cotangent, weight_in, weight_down, swap_flag):
    row_count = tokens.shape[0]
    model_width = tokens.shape[1]
    per_device = weight_in.shape[0]
    groups = lax.axis_size("expert")
    replicas = lax.axis_size("dp")
    part_width = model_width // replicas
    device_ids = jnp.arange(groups, dtype=jnp.int32)
    my_index = lax.axis_index("expert")
    my_flag = jnp.sum(jnp.where(device_ids == my_index, swap_flag, 0))
    expert_range = jnp.arange(EXPERTS, dtype=jnp.int32)
    home_device = expert_range // per_device
    moved_flag = jnp.sum(
        jnp.where(home_device[:, None] == device_ids[None, :], swap_flag[None, :], 0), axis=1
    )
    target_device = jnp.bitwise_xor(home_device, 2 * moved_flag)
    dest_place = target_device * per_device + expert_range % per_device

    onehot = expert_ids[:, :, None] == expert_range[None, None, :]
    named = jnp.sum(onehot.astype(jnp.bfloat16), axis=1)
    token_range = jnp.arange(row_count, dtype=jnp.int32)
    earlier = (token_range[:, None] > token_range[None, :]).astype(jnp.bfloat16)
    rank_table = jnp.dot(earlier, named, preferred_element_type=jnp.float32).astype(jnp.int32)
    slot_rank = jnp.sum(jnp.where(onehot, rank_table[:, None, :], 0), axis=2)
    place_of = jnp.sum(jnp.where(onehot, dest_place[None, None, :], 0), axis=2)
    slot_index = (expert_ids * CAP + slot_rank).reshape(-1)

    my_replica = lax.axis_index("dp")
    part_index = (place_of * replicas + my_replica) * CAP + slot_rank
    route = jnp.concatenate([part_index.astype(jnp.float32), gate_probs], axis=1)
    route = lax.all_gather(route, "dp", axis=0, tiled=True)
    part_index = route[:, :TOP].astype(jnp.int32).reshape(-1)
    part_probs = route[:, TOP:]
    both = jnp.stack([tokens, cotangent])
    both = lax.all_to_all(both, "dp", split_axis=2, concat_axis=1, tiled=True)

    token_copies = jnp.repeat(tokens, TOP, axis=0)
    grad_rows = (gate_probs[:, :, None] * cotangent[:, None, :].astype(jnp.float32)).astype(
        jnp.bfloat16
    )
    grad_rows = grad_rows.reshape(row_count * TOP, model_width)
    empty_rows = jnp.zeros((EXPERTS * CAP, model_width), jnp.bfloat16)
    send_x = (
        empty_rows.at[slot_index].set(token_copies).reshape(groups, per_device, CAP, model_width)
    )
    send_grad = (
        empty_rows.at[slot_index].set(grad_rows).reshape(groups, per_device, CAP, model_width)
    )
    recv_x = lax.all_to_all(send_x, "expert", split_axis=0, concat_axis=0, tiled=True)
    recv_grad = lax.all_to_all(send_grad, "expert", split_axis=0, concat_axis=0, tiled=True)

    part_x = jnp.repeat(both[0], TOP, axis=0)
    part_grad = (part_probs[:, :, None] * both[1][:, None, :].astype(jnp.float32)).astype(
        jnp.bfloat16
    )
    part_grad = part_grad.reshape(replicas * row_count * TOP, part_width)
    part_rows = jnp.concatenate([part_x, part_grad], axis=1)
    send_part = (
        jnp.zeros((EXPERTS * replicas * CAP, 2 * part_width), jnp.bfloat16)
        .at[part_index]
        .set(part_rows)
        .reshape(groups, per_device, replicas, CAP, 2 * part_width)
    )
    recv_part = lax.all_to_all(send_part, "expert", split_axis=0, concat_axis=0, tiled=True)

    projected = jnp.einsum("nscd,sdf->nscf", recv_x, weight_in, preferred_element_type=jnp.float32)
    pre_gate = projected[..., :FF]
    up_part = projected[..., FF:]
    sigmoid_gate = jax.nn.sigmoid(pre_gate)
    activated = pre_gate * sigmoid_gate
    hidden = (activated * up_part).astype(jnp.bfloat16)
    hidden_moved = jnp.where(my_flag == 1, swapped(hidden, "expert", 1), hidden)
    hidden_all = lax.all_gather(hidden_moved, "dp", axis=0)
    expert_out = jnp.einsum(
        "nscf,sfd->nscd", hidden, weight_down, preferred_element_type=jnp.float32
    ).astype(jnp.bfloat16)
    hidden_grad = jnp.einsum(
        "nscd,sfd->nscf", recv_grad, weight_down, preferred_element_type=jnp.float32
    )
    gate_grad = hidden_grad * up_part * sigmoid_gate * (1.0 + pre_gate * (1.0 - sigmoid_gate))
    proj_grad = jnp.concatenate([gate_grad, hidden_grad * activated], axis=-1).astype(jnp.bfloat16)
    proj_moved = jnp.where(my_flag == 1, swapped(proj_grad, "expert", 1), proj_grad)
    proj_all = lax.all_gather(proj_moved, "dp", axis=0)
    row_grad = jnp.einsum(
        "nscf,sdf->nscd", proj_grad, weight_in, preferred_element_type=jnp.float32
    ).astype(jnp.bfloat16)
    home_out = lax.all_to_all(expert_out, "expert", split_axis=0, concat_axis=0, tiled=True)
    home_grad = lax.all_to_all(row_grad, "expert", split_axis=0, concat_axis=0, tiled=True)

    grad_first = jnp.einsum(
        "nsrcd,rnscf->sdf",
        recv_part[..., :part_width],
        proj_all,
        preferred_element_type=jnp.float32,
    )
    grad_second = jnp.einsum(
        "rnscf,nsrcd->sfd",
        hidden_all,
        recv_part[..., part_width:],
        preferred_element_type=jnp.float32,
    )

    out_rows = home_out.reshape(EXPERTS * CAP, model_width)[slot_index]
    out_rows = out_rows.astype(jnp.float32).reshape(row_count, TOP, model_width)
    layer_out = jnp.sum(gate_probs[:, :, None] * out_rows, axis=1).astype(jnp.bfloat16)
    gate_grads = jnp.sum(cotangent[:, None, :].astype(jnp.float32) * out_rows, axis=2)
    back_rows = home_grad.reshape(EXPERTS * CAP, model_width)[slot_index]
    back_rows = back_rows.astype(jnp.float32).reshape(row_count, TOP, model_width)
    token_grads = jnp.sum(back_rows, axis=1).astype(jnp.bfloat16)
    return (layer_out, gate_grads, token_grads, grad_first, grad_second)


def solution(mesh):
    in_specs = (
        P(("expert", "dp"), None),
        P(("expert", "dp"), None),
        P(("expert", "dp"), None),
        P(("expert", "dp"), None),
        P("expert", None, None),
        P("expert", None, None),
        P(),
    )
    out_specs = (
        P(("expert", "dp"), None),
        P(("expert", "dp"), None),
        P(("expert", "dp"), None),
        P("expert", "dp", None),
        P("expert", None, "dp"),
    )
    return jax.shard_map(body, mesh=mesh, in_specs=in_specs, out_specs=out_specs, check_vma=False)
```

time: 1620 us -> 591 us (0.36)
  waiting for transfers between devices: 1280 us -> 190 us
  local copies, waits for them, and re-layouts: 124 us -> 174 us
    all_to_all x1, waiting for transfers between devices: 515 us -> 32 us  [body(): lax.all_to_all(send_x, 'expert', split_axis=0, concat_axis=0, tiled=True)]
    reduce_scatter x2 -> x0, waiting for transfers between devices: 406 us -> none  [the longest x1 406 us: body(): lax.psum_scatter(grad_first.astype(jnp.bfloat16), 'dp', scatter_dimension...]
    all_to_all x1, waiting for transfers between devices: 304 us -> 36.4 us  [body(): lax.all_to_all(send_grad, 'expert', split_axis=0, concat_axis=0, tiled=True)]
    all_gather x0 -> x2, waiting for transfers between devices: none -> 37.9 us  [the longest x1 37.9 us: body(): proj_all = lax.all_gather(proj_moved, 'dp', axis=0)]
    all_to_all x0 -> x2, waiting for transfers between devices: none -> 36.1 us  [the longest x1 36.1 us: body(): lax.all_to_all(send_part, 'expert', split_axis=0, concat_axis=0, tiled=True)]
    reshape x0 -> x5, local copies, waits for them, and re-layouts: none -> 31.9 us  [the longest x2 29 us: body(): send_part = jnp.zeros((EXPERTS * replicas * CAP, 2 * part_width), jnp.bfl...]
    scatter x0 -> x1, other arithmetic: none -> 25.6 us  [body(): send_part = jnp.zeros((EXPERTS * replicas * CAP, 2 * part_width), jnp.bfl...]
    all_to_all x1, waiting for transfers between devices: 24.1 us -> 0.01 us  [body(): lax.all_to_all(row_grad, 'expert', split_axis=0, concat_axis=0, tiled=True)]
  transfers between devices with their start and end apart: 8 -> 10, of which waited for: 5 -> 7; matrix products, arithmetic and copies ran while one was open for 15% -> 49% of each run, Pallas kernels for 0% -> 0%
where the time goes in v1:
time: 591 us; the launch traced here: 582 us
  waiting for transfers between devices  190 us (32%)
  local copies, waits for them, and re-layouts  174 us (29%)
  matrix products  94.3 us (16%)
  other arithmetic  61.1 us (10%)
  starting transfers between devices  33.6 us (6%)
  between operations  15.4 us (3%)
  blocking collectives  13.8 us (2%)
    all_gather x1, waiting for transfers between devices, body(): proj_all = lax.all_gather(proj_moved, 'dp', axis=0)  37.9 us
    all_to_all x1, waiting for transfers between devices, body(): lax.all_to_all(send_grad, 'expert', split_axis=0, concat_axis=0, tiled=True)  36.4 us
    all_to_all x1, waiting for transfers between devices, body(): lax.all_to_all(send_part, 'expert', split_axis=0, concat_axis=0, tiled=True)  36.1 us
    all_to_all x1, waiting for transfers between devices, body(): lax.all_to_all(send_x, 'expert', split_axis=0, concat_axis=0, tiled=True)  32 us
    reshape x2, local copies, waits for them, and re-layouts, body(): send_part = jnp.zeros((EXPERTS * replicas * CAP, 2 * part_width), jnp.bfl...  29 us
    all_to_all x1, waiting for transfers between devices, body(): lax.all_to_all(expert_out, 'expert', split_axis=0, concat_axis=0, tiled=T...  25.7 us
    scatter x1, other arithmetic, body(): send_part = jnp.zeros((EXPERTS * replicas * CAP, 2 * part_width), jnp.bfl...  25.6 us
    dot_general x1, matrix products, body(): jnp.einsum('nscf,sdf->nscd', proj_grad, weight_in, preferred_element_type...  23.2 us
  transfers between devices with their start and end apart: 10, of which 7 were waited for; matrix products, arithmetic and copies ran while one was open for 49% of the time, Pallas kernels for 0%

profile of v1, /device:TPU:0, one launch (start us, length us, event | category | flops | bytes accessed | tf_op | source)
XLA Modules:
  0.0 581.8 jit_solution(14033323667888095273)
XLA Ops:
  10.5 10.1 %scatter_custom_fusion = bf16[1280,2048]{1,0:T(8,128)(2,1)} fusion(s32[1024]{0:T(1024)S(1)} %bitcast.86, bf16[]{:T(256)} %constant.49.clone.1, bf16[128,2048]{1,0:T(8,128)(2,1)} %param.7), kind=kCustom, calls=%fused_computation.39 | custom fusion | bytes 5767170 | tf_op jit(solution)/shard_map/scatter | solution.py:65
  20.6 8.9 %reshape.177 = bf16[8,8,20,2048]{3,2,1,0:T(8,128)(2,1)} reshape(bf16[1280,2048]{1,0:T(8,128)(2,1)} %scatter_custom_fusion) | data formatting | bytes 10485760 | tf_op jit(solution)/shard_map/reshape | solution.py:65
  29.5 8.5 %copy.110 = bf16[8,8,20,2048]{3,1,2,0:T(8,128)(2,1)} copy(bf16[8,8,20,2048]{3,2,1,0:T(8,128)(2,1)} %reshape.177) | data formatting | bytes 10485760 | tf_op jit(solution)/shard_map/reshape | solution.py:65
  44.6 10.0 %scatter_custom_fusion.1 = bf16[1280,2048]{1,0:T(8,128)(2,1)} fusion(s32[1024]{0:T(1024)S(1)} %bitcast.87, f32[1024]{0:T(1024)S(1)} %mul.112, f32[128,2048]{1,0:T(8,128)S(1)} %convert_element_type.80, bf16[]{:T(256)} %constant.49.clone.1), kind=kCustom, calls=%fused_computation.37 | custom fusion | flops 4194304 | bytes 6295554 | tf_op jit(solution)/shard_map/scatter | solution.py:68
  54.6 8.9 %reshape.179 = bf16[8,8,20,2048]{3,2,1,0:T(8,128)(2,1)} reshape(bf16[1280,2048]{1,0:T(8,128)(2,1)} %scatter_custom_fusion.1) | data formatting | bytes 10485760 | tf_op jit(solution)/shard_map/reshape | solution.py:68
  63.5 8.5 %copy.115 = bf16[8,8,20,2048]{3,1,2,0:T(8,128)(2,1)} copy(bf16[8,8,20,2048]{3,2,1,0:T(8,128)(2,1)} %reshape.179) | data formatting | bytes 10485760 | tf_op jit(solution)/shard_map/reshape | solution.py:68
  72.1 32.0 %all-to-all-done = bf16[8,8,20,2048]{3,1,2,0:T(8,128)(2,1)} async-done(((bf16[8,8,20,2048]{3,1,2,0:T(8,128)(2,1)}), bf16[8,8,20,2048]{3,1,2,0:T(8,128)(2,1)}, u32[]{:S(2)}, u32[]{:S(2)}) %all-to-all-start) | async-done | bytes 5242912 | tf_op jit(solution)/shard_map/all_to_all | solution.py:70
  111.3 21.8 %fusion.52 = f32[8,8,20,768]{3,2,0,1:T(8,128)} fusion(bf16[8,2048,768]{2,1,0:T(8,128)(2,1)} %param.11, bf16[8,8,20,2048]{3,1,2,0:T(8,128)(2,1)} %all-to-all-done), kind=kOutput, calls=%fused_computation.57 | convolution fusion | flops 4026531840 | bytes 34340864 | tf_op jit(solution)/shard_map/nscd,sdf->nscf/dot_general | solution.py:87
  133.1 36.4 %all-to-all-done.2 = bf16[8,8,20,2048]{3,1,2,0:T(8,128)(2,1)} async-done(((bf16[8,8,20,2048]{3,1,2,0:T(8,128)(2,1)}), bf16[8,8,20,2048]{3,1,2,0:T(8,128)(2,1)}, u32[]{:S(2)}, u32[]{:S(2)}) %all-to-all-start.2) | async-done | bytes 5242912 | tf_op jit(solution)/shard_map/all_to_all | solution.py:71
  175.4 17.2 %fusion.49 = (bf16[8,8,20,384]{3,2,0,1:T(8,128)(2,1)S(1)}, bf16[8,8,20,384]{3,2,0,1:T(8,128)(2,1)S(1)}, bf16[8,8,20,384]{3,2,0,1:T(8,128)(2,1)S(1)}) fusion(f32[8,8,20,768]{3,2,0,1:T(8,128)} %fusion.52, bf16[8,384,2048]{2,1,0:T(8,128)(2,1)} %param.12, bf16[8,8,20,2048]{3,1,2,0:T(8,128)(2,1)} %all-to-all-done.2), kind=kOutput, calls=%fused_computation.51 | convolution fusion | flops 2020638720 | bytes 24707072 | tf_op jit(solution)/shard_map/nscd,sfd->nscf/dot_general | solution.py:98
  192.6 8.0 %convert_bitcast_fusion.1 = bf16[8,8,20,2048]{3,2,0,1:T(8,128)(2,1)S(1)} fusion(bf16[8,8,20,384]{3,2,0,1:T(8,128)(2,1)S(1)} %get-tuple-element.28, bf16[8,384,2048]{2,1,0:T(8,128)(2,1)} %param.12), kind=kOutput, calls=%fused_computation.33 | convolution fusion | flops 2015887360 | bytes 18808832 | tf_op jit(solution)/shard_map/nscf,sfd->nscd/dot_general | solution.py:95
  214.6 23.2 %convert_bitcast_fusion = bf16[8,8,20,2048]{3,2,0,1:T(8,128)(2,1)} fusion(bf16[8,2048,768]{2,1,0:T(8,128)(2,1)} %param.11, bf16[8,8,20,384]{3,2,0,1:T(8,128)(2,1)S(1)} %get-tuple-element.27, bf16[8,8,20,384]{3,2,0,1:T(8,128)(2,1)S(1)} %get-tuple-element.26), kind=kOutput, calls=%fused_computation.32 | convolution fusion | flops 4033085440 | bytes 32374784 | tf_op jit(solution)/shard_map/nscf,sdf->nscd/dot_general | solution.py:105
  237.8 8.5 %copy.117 = bf16[8,8,20,2048]{3,1,2,0:T(8,128)(2,1)} copy(bf16[8,8,20,2048]{3,2,0,1:T(8,128)(2,1)} %convert_bitcast_fusion) | data formatting | bytes 10485760 | tf_op jit(solution)/shard_map/convert_element_type | solution.py:107
  246.2 25.7 %all-to-all-done.1 = bf16[8,8,20,2048]{3,1,2,0:T(8,128)(2,1)} async-done(((bf16[8,8,20,2048]{3,1,2,0:T(8,128)(2,1)}), bf16[8,8,20,2048]{3,1,2,0:T(8,128)(2,1)}, u32[]{:S(2)}, u32[]{:S(2)}) %all-to-all-start.1) | async-done | bytes 5242912 | tf_op jit(solution)/shard_map/all_to_all | solution.py:108
  277.9 14.1 %collective-permute-done.1 = bf16[8,8,20,384]{3,1,2,0:T(8,128)(2,1)} collective-permute-done((bf16[8,8,20,384]{3,1,2,0:T(8,128)(2,1)}, bf16[8,8,20,384]{3,1,2,0:T(8,128)(2,1)}, u32[]{:S(2)}, u32[]{:S(2)}) %collective-permute-start.1) | collective-permute-done | bytes 983072 | tf_op jit(solution)/shard_map/ppermute | solution.py:19
  294.6 13.8 %all_gather.15 = f32[512,16]{0,1:T(8,128)S(1)} all-gather(f32[128,16]{0,1:T(8,128)S(1)} %pad_maximum_fusion.2), channel_id=1, replica_groups=mesh['expert'=8,'dp'=4] {'dp'}, dimensions={0}, use_global_device_ids=true | all-gather | bytes 40960 | tf_op jit(solution)/shard_map/all_gather | solution.py:52
  322.9 25.6 %scatter_custom_fusion.2 = bf16[5120,1024]{1,0:T(8,128)(2,1)} fusion(s32[4096]{0:T(1024)S(1)} %bitcast.85, bf16[4096,512]{1,0:T(8,128)(2,1)} %fusion.16, bf16[]{:T(256)} %constant.66, bf16[4096,512]{1,0:T(8,128)(2,1)} %broadcast_bitcast_fusion, bf16[]{:T(256)} %constant.49.clone.1), kind=kCustom, calls=%fused_computation.19 | custom fusion | flops 16777216 | bytes 18874372 | tf_op jit(solution)/shard_map/scatter | solution.py:82
  348.5 16.4 %reshape.183 = bf16[8,8,4,20,1024]{4,3,2,1,0:T(8,128)(2,1)} reshape(bf16[5120,1024]{1,0:T(8,128)(2,1)} %scatter_custom_fusion.2) | data formatting | bytes 20971520 | tf_op jit(solution)/shard_map/reshape | solution.py:83
  364.9 12.7 %copy.125 = bf16[8,8,4,20,1024]{4,1,3,2,0:T(8,128)(2,1)} copy(bf16[8,8,4,20,1024]{4,3,2,1,0:T(8,128)(2,1)} %reshape.183) | data formatting | bytes 20971520 | tf_op jit(solution)/shard_map/reshape | solution.py:83
  382.8 7.6 %collective-permute-done = bf16[8,8,20,768]{3,1,2,0:T(8,128)(2,1)} collective-permute-done((bf16[8,8,20,768]{3,1,2,0:T(8,128)(2,1)}, bf16[8,8,20,768]{3,1,2,0:T(8,128)(2,1)}, u32[]{:S(2)}, u32[]{:S(2)}) %collective-permute-start) | collective-permute-done | bytes 1966112 | tf_op jit(solution)/shard_map/ppermute | solution.py:19
  394.1 9.2 %copy.113 = bf16[8,8,20,2048]{3,2,1,0:T(8,128)(2,1)} copy(bf16[8,8,20,2048]{3,1,2,0:T(8,128)(2,1)} %all-to-all-done.1) | data formatting | bytes 10485760 | tf_op jit(solution)/shard_map/all_to_all | solution.py:108
  403.3 9.5 %reshape.178 = bf16[1280,2048]{1,0:T(8,128)(2,1)} reshape(bf16[8,8,20,2048]{3,2,1,0:T(8,128)(2,1)} %copy.113) | data formatting | bytes 10485760 | tf_op jit(solution)/shard_map/reshape | solution.py:124
  412.8 12.1 %gather_fusion = bf16[1024,2048]{1,0:T(8,128)(2,1)} fusion(bf16[1280,2048]{1,0:T(8,128)(2,1)} %reshape.178, s32[1024]{0:T(1024)S(1)} %broadcast_clamp_fusion), kind=kCustom, calls=%fused_computation | custom fusion | bytes 8392704 | tf_op jit(solution)/shard_map/gather | solution.py:124
  431.2 8.8 %copy.118 = bf16[8,8,20,2048]{3,2,1,0:T(8,128)(2,1)} copy(bf16[8,8,20,2048]{3,1,2,0:T(8,128)(2,1)} %all-to-all-done.3) | data formatting | bytes 10485760 | tf_op jit(solution)/shard_map/all_to_all | solution.py:109
  440.0 9.0 %reshape.180 = bf16[1280,2048]{1,0:T(8,128)(2,1)} reshape(bf16[8,8,20,2048]{3,2,1,0:T(8,128)(2,1)} %copy.118) | data formatting | bytes 10485760 | tf_op jit(solution)/shard_map/reshape | solution.py:128
  449.0 12.2 %gather_fusion.1 = bf16[1024,2048]{1,0:T(8,128)(2,1)} fusion(bf16[1280,2048]{1,0:T(8,128)(2,1)} %reshape.180, s32[1024]{0:T(1024)S(1)} %broadcast_clamp_fusion), kind=kCustom, calls=%fused_computation.1 | custom fusion | bytes 8392704 | tf_op jit(solution)/shard_map/gather | solution.py:128
  461.3 5.9 %bitcast_reduce_fusion = bf16[128,2048]{1,0:T(8,128)(2,1)} fusion(bf16[1024,2048]{1,0:T(8,128)(2,1)} %gather_fusion.1), kind=kLoop, calls=%fused_computation.38 | loop fusion | flops 1835008 | bytes 4718592 | tf_op jit(solution)/shard_map/reduce_sum | solution.py:130
  467.2 36.1 %all-to-all-done.5 = bf16[8,8,4,20,1024]{4,1,3,2,0:T(8,128)(2,1)} async-done(((bf16[8,8,4,20,1024]{4,1,3,2,0:T(8,128)(2,1)}), bf16[8,8,4,20,1024]{4,1,3,2,0:T(8,128)(2,1)}, u32[]{:S(2)}, u32[]{:S(2)}) %all-to-all-start.5) | async-done | bytes 10485792 | tf_op jit(solution)/shard_map/all_to_all | solution.py:85
  503.3 9.5 %fusion.62 = (bf16[8,8,4,20,512]{4,1,3,2,0:T(8,128)(2,1)}, bf16[8,8,4,20,512]{4,1,3,2,0:T(8,128)(2,1)}) fusion(bf16[8,8,4,20,1024]{4,1,3,2,0:T(8,128)(2,1)} %all-to-all-done.5), kind=kLoop, calls=%fused_computation.87 | loop fusion | bytes 20971520 | tf_op jit(solution)/shard_map/slice | solution.py:120
  512.7 11.0 %fusion.40 = f32[8,384,512]{2,1,0:T(8,128)} fusion(bf16[8,8,4,20,512]{4,1,3,2,0:T(8,128)(2,1)} %get-tuple-element.24, bf16[4,8,8,20,384]{4,3,1,0,2:T(8,128)(2,1)} %bitcast.90), kind=kOutput, calls=%fused_computation.43 | convolution fusion | flops 2013265920 | bytes 15466496 | tf_op jit(solution)/shard_map/rnscf,nsrcd->sfd/dot_general | solution.py:117
  523.8 37.9 %all-gather.5.cloned.1.call-done = bf16[32,8,20,768]{3,2,0,1:T(8,128)(2,1)} async-done(((bf16[8,8,20,768]{3,2,0,1:T(8,128)(2,1)}), bf16[32,8,20,768]{3,2,0,1:T(8,128)(2,1)}) %all-gather.5.cloned.1.call-update) | async-done | bytes 7864336 | tf_op jit(solution)/shard_map/all_gather | solution.py:104
  561.7 12.9 %fusion.29 = f32[8,512,768]{2,1,0:T(8,128)} fusion(bf16[4,8,8,20,768]{4,3,1,0,2:T(8,128)(2,1)} %bitcast.89, bf16[8,8,4,20,512]{4,1,3,2,0:T(8,128)(2,1)} %get-tuple-element.25), kind=kOutput, calls=%fused_computation.36 | convolution fusion | flops 4026531840 | bytes 25690112 | tf_op jit(solution)/shard_map/nsrcd,rnscf->sdf/dot_general | solution.py:111
  (71 shorter events, 74.5 us)
Async XLA Ops:
  38.1 5.6 copy-start.7
  38.1 6.4 %copy-start.4 = (bf16[128,2048]{1,0:T(8,128)(2,1)S(1)}, bf16[128,2048]{1,0:T(8,128)(2,1)}, u32[]{:S(2)}) copy-start(bf16[128,2048]{1,0:T(8,128)(2,1)} %param.10) | copy-start | bytes 1572868
  38.1 66.0 %all-to-all-start = ((bf16[8,8,20,2048]{3,1,2,0:T(8,128)(2,1)}), bf16[8,8,20,2048]{3,1,2,0:T(8,128)(2,1)}, u32[]{:S(2)}, u32[]{:S(2)}) async-start(bf16[8,8,20,2048]{3,1,2,0:T(8,128)(2,1)} %copy.110), calls=%async_computation | async-start | bytes 10485760 | tf_op jit(solution)/shard_map/all_to_all | solution.py:70
  43.7 0.6 copy-start.5
  44.6 19.0 %copy-start = (f32[128,2048]{1,0:T(8,128)}, f32[128,2048]{1,0:T(8,128)S(1)}, u32[]{:S(2)}) copy-start(f32[128,2048]{1,0:T(8,128)S(1)} %convert_element_type.80) | copy-start | bytes 3145732
  72.0 37.1 %copy-start.3 = (bf16[128,2048]{1,0:T(8,128)(2,1)S(1)}, bf16[128,2048]{1,0:T(8,128)(2,1)}, u32[]{:S(2)}) copy-start(bf16[128,2048]{1,0:T(8,128)(2,1)} %param.7) | copy-start | bytes 1572868
  104.1 65.5 %all-to-all-start.2 = ((bf16[8,8,20,2048]{3,1,2,0:T(8,128)(2,1)}), bf16[8,8,20,2048]{3,1,2,0:T(8,128)(2,1)}, u32[]{:S(2)}, u32[]{:S(2)}) async-start(bf16[8,8,20,2048]{3,1,2,0:T(8,128)(2,1)} %copy.115), calls=%async_computation.2 | async-start | bytes 10485760 | tf_op jit(solution)/shard_map/all_to_all | solution.py:71
  169.5 36.5 %all-to-all-start.4 = ((bf16[2,128,2048]{1,0,2:T(2,128)(2,1)}), bf16[2,128,2048]{1,0,2:T(2,128)(2,1)}, u32[]{:S(2)}, u32[]{:S(2)}) async-start(bf16[2,128,2048]{1,0,2:T(2,128)(2,1)} %copy.120), calls=%async_computation.4 | async-start | bytes 2097152 | tf_op jit(solution)/shard_map/all_to_all | solution.py:56
  206.0 65.9 %all-to-all-start.1 = ((bf16[8,8,20,2048]{3,1,2,0:T(8,128)(2,1)}), bf16[8,8,20,2048]{3,1,2,0:T(8,128)(2,1)}, u32[]{:S(2)}, u32[]{:S(2)}) async-start(bf16[8,8,20,2048]{3,1,2,0:T(8,128)(2,1)} %copy.112), calls=%async_computation.1 | async-start | bytes 10485760 | tf_op jit(solution)/shard_map/all_to_all | solution.py:108
  212.6 79.4 %collective-permute-start.1 = (bf16[8,8,20,384]{3,1,2,0:T(8,128)(2,1)}, bf16[8,8,20,384]{3,1,2,0:T(8,128)(2,1)}, u32[]{:S(2)}, u32[]{:S(2)}) collective-permute-start(bf16[8,8,20,384]{3,1,2,0:T(8,128)(2,1)} %copy.130), channel_id=1, source_target_pairs={{0,8},{8,0},{4,12},{12,4},{16,24},{24,16},{20,28},{28,20},{1,9},{9... | collective-permute-start | bytes 2949128 | tf_op jit(solution)/shard_map/ppermute | solution.py:19
  246.2 30.4 %copy-start.8 = (s32[8]{0:T(128)S(1)}, s32[8]{0:T(128)}, u32[]{:S(2)}) copy-start(s32[8]{0:T(128)} %param.13) | copy-start | bytes 100
  271.9 105.6 %all-to-all-start.3 = ((bf16[8,8,20,2048]{3,1,2,0:T(8,128)(2,1)}), bf16[8,8,20,2048]{3,1,2,0:T(8,128)(2,1)}, u32[]{:S(2)}, u32[]{:S(2)}) async-start(bf16[8,8,20,2048]{3,1,2,0:T(8,128)(2,1)} %copy.117), calls=%async_computation.3 | async-start | bytes 10485760 | tf_op jit(solution)/shard_map/all_to_all | solution.py:109
  276.6 236.2 %all-gather.7.cloned.1.call-start = ((), (), s32[]{:S(2)}) async-start(), calls=%async_computation.7 | async-start | bytes 5898240 | tf_op jit(solution)/shard_map/all_gather | solution.py:94
  317.6 2.8 copy-start.2
  320.3 70.1 %collective-permute-start = (bf16[8,8,20,768]{3,1,2,0:T(8,128)(2,1)}, bf16[8,8,20,768]{3,1,2,0:T(8,128)(2,1)}, u32[]{:S(2)}, u32[]{:S(2)}) collective-permute-start(bf16[8,8,20,768]{3,1,2,0:T(8,128)(2,1)} %copy.127), channel_id=1, source_target_pairs={{0,8},{8,0},{4,12},{12,4},{16,24},{24,16},{20,28},{28,20},{1,9},{9... | collective-permute-start | bytes 5898248 | tf_op jit(solution)/shard_map/ppermute | solution.py:19
  377.6 125.7 %all-to-all-start.5 = ((bf16[8,8,4,20,1024]{4,1,3,2,0:T(8,128)(2,1)}), bf16[8,8,4,20,1024]{4,1,3,2,0:T(8,128)(2,1)}, u32[]{:S(2)}, u32[]{:S(2)}) async-start(bf16[8,8,4,20,1024]{4,1,3,2,0:T(8,128)(2,1)} %copy.125), calls=%async_computation.5 | async-start | bytes 20971520 | tf_op jit(solution)/shard_map/all_to_all | solution.py:85
  382.7 178.9 %all-gather.5.cloned.1.call-start = ((), (), s32[]{:S(2)}) async-start(), calls=%async_computation.6 | async-start | bytes 11796480 | tf_op jit(solution)/shard_map/all_gather | solution.py:104
  412.8 12.1 %copy-start.1 = (f32[128,2048]{1,0:T(8,128)S(1)}, f32[128,2048]{1,0:T(8,128)}, u32[]{:S(2)}) copy-start(f32[128,2048]{1,0:T(8,128)} %copy-done) | copy-start | bytes 3145732
  412.8 12.1 %copy-start.6 = (f32[128,8]{1,0:T(8,128)S(1)}, f32[128,8]{1,0:T(8,128)}, u32[]{:S(2)}) copy-start(f32[128,8]{1,0:T(8,128)} %copy-done.5) | copy-start | bytes 12292
Sparse Core Ops, SparseCore 0:
  294.7 90.0 all-gather.6
  394.2 167.3 all-gather.4

commit v2 on v1

--- a/solution.py
+++ b/solution.py
@@ -44,14 +44,16 @@
     rank_table = jnp.dot(earlier, named, preferred_element_type=jnp.float32).astype(jnp.int32)
     slot_rank = jnp.sum(jnp.where(onehot, rank_table[:, None, :], 0), axis=2)
     place_of = jnp.sum(jnp.where(onehot, dest_place[None, None, :], 0), axis=2)
-    slot_index = (expert_ids * CAP + slot_rank).reshape(-1)
+    slot_index = (expert_ids // per_device * CAP + slot_rank) * per_device
+    slot_index = (slot_index + expert_ids % per_device).reshape(-1)
 
     my_replica = lax.axis_index("dp")
-    part_index = (place_of * replicas + my_replica) * CAP + slot_rank
+    part_index = (place_of // per_device * replicas + my_replica) * CAP + slot_rank
+    part_index = part_index * per_device + place_of % per_device
     route = jnp.concatenate([part_index.astype(jnp.float32), gate_probs], axis=1)
-    route = lax.all_gather(route, "dp", axis=0, tiled=True)
-    part_index = route[:, :TOP].astype(jnp.int32).reshape(-1)
-    part_probs = route[:, TOP:]
+    route = jnp.broadcast_to(route[None], (replicas,) + route.shape)
+    route = lax.all_to_all(route, "dp", split_axis=0, concat_axis=0, tiled=True)
+    route = route.reshape(replicas * row_count, 2 * TOP)
     both = jnp.stack([tokens, cotangent])
     both = lax.all_to_all(both, "dp", split_axis=2, concat_axis=1, tiled=True)
 
@@ -62,14 +64,17 @@
     grad_rows = grad_rows.reshape(row_count * TOP, model_width)
     empty_rows = jnp.zeros((EXPERTS * CAP, model_width), jnp.bfloat16)
     send_x = (
-        empty_rows.at[slot_index].set(token_copies).reshape(groups, per_device, CAP, model_width)
+        empty_rows.at[slot_index].set(token_copies).reshape(groups, CAP, per_device, model_width)
     )
     send_grad = (
-        empty_rows.at[slot_index].set(grad_rows).reshape(groups, per_device, CAP, model_width)
+        empty_rows.at[slot_index].set(grad_rows).reshape(groups, CAP, per_device, model_width)
     )
+    send_x, both, route = lax.optimization_barrier((send_x, both, route))
     recv_x = lax.all_to_all(send_x, "expert", split_axis=0, concat_axis=0, tiled=True)
     recv_grad = lax.all_to_all(send_grad, "expert", split_axis=0, concat_axis=0, tiled=True)
 
+    part_index = route[:, :TOP].astype(jnp.int32).reshape(-1)
+    part_probs = route[:, TOP:]
     part_x = jnp.repeat(both[0], TOP, axis=0)
     part_grad = (part_probs[:, :, None] * both[1][:, None, :].astype(jnp.float32)).astype(
         jnp.bfloat16
@@ -80,42 +85,49 @@
         jnp.zeros((EXPERTS * replicas * CAP, 2 * part_width), jnp.bfloat16)
         .at[part_index]
         .set(part_rows)
-        .reshape(groups, per_device, replicas, CAP, 2 * part_width)
+        .reshape(groups, replicas, CAP, per_device, 2 * part_width)
     )
-    recv_part = lax.all_to_all(send_part, "expert", split_axis=0, concat_axis=0, tiled=True)
 
-    projected = jnp.einsum("nscd,sdf->nscf", recv_x, weight_in, preferred_element_type=jnp.float32)
+    projected = jnp.einsum("ncsd,sdf->ncsf", recv_x, weight_in, preferred_element_type=jnp.float32)
     pre_gate = projected[..., :FF]
     up_part = projected[..., FF:]
     sigmoid_gate = jax.nn.sigmoid(pre_gate)
     activated = pre_gate * sigmoid_gate
     hidden = (activated * up_part).astype(jnp.bfloat16)
     hidden_moved = jnp.where(my_flag == 1, swapped(hidden, "expert", 1), hidden)
+    hidden_moved, send_part, recv_grad = lax.optimization_barrier(
+        (hidden_moved, send_part, recv_grad)
+    )
     hidden_all = lax.all_gather(hidden_moved, "dp", axis=0)
     expert_out = jnp.einsum(
-        "nscf,sfd->nscd", hidden, weight_down, preferred_element_type=jnp.float32
+        "ncsf,sfd->ncsd", hidden, weight_down, preferred_element_type=jnp.float32
     ).astype(jnp.bfloat16)
     hidden_grad = jnp.einsum(
-        "nscd,sfd->nscf", recv_grad, weight_down, preferred_element_type=jnp.float32
+        "ncsd,sfd->ncsf", recv_grad, weight_down, preferred_element_type=jnp.float32
     )
     gate_grad = hidden_grad * up_part * sigmoid_gate * (1.0 + pre_gate * (1.0 - sigmoid_gate))
     proj_grad = jnp.concatenate([gate_grad, hidden_grad * activated], axis=-1).astype(jnp.bfloat16)
     proj_moved = jnp.where(my_flag == 1, swapped(proj_grad, "expert", 1), proj_grad)
-    proj_all = lax.all_gather(proj_moved, "dp", axis=0)
     row_grad = jnp.einsum(
-        "nscf,sdf->nscd", proj_grad, weight_in, preferred_element_type=jnp.float32
+        "ncsf,sdf->ncsd", proj_grad, weight_in, preferred_element_type=jnp.float32
     ).astype(jnp.bfloat16)
     home_out = lax.all_to_all(expert_out, "expert", split_axis=0, concat_axis=0, tiled=True)
+    proj_moved, hidden_all, row_grad, send_part = lax.optimization_barrier(
+        (proj_moved, hidden_all, row_grad, send_part)
+    )
+    proj_all = lax.all_gather(proj_moved, "dp", axis=0)
+    recv_part = lax.all_to_all(send_part, "expert", split_axis=0, concat_axis=0, tiled=True)
     home_grad = lax.all_to_all(row_grad, "expert", split_axis=0, concat_axis=0, tiled=True)
+    proj_all, home_grad = lax.optimization_barrier((proj_all, home_grad))
 
     grad_first = jnp.einsum(
-        "nsrcd,rnscf->sdf",
+        "nrcsd,rncsf->sdf",
         recv_part[..., :part_width],
         proj_all,
         preferred_element_type=jnp.float32,
     )
     grad_second = jnp.einsum(
-        "rnscf,nsrcd->sfd",
+        "rncsf,nrcsd->sfd",
         hidden_all,
         recv_part[..., part_width:],
         preferred_element_type=jnp.float32,

time: 591 us -> 565 us (0.956)
  local copies, waits for them, and re-layouts: 174 us -> 68.7 us
  waiting for transfers between devices: 190 us -> 262 us
  other arithmetic: 61.1 us -> 77.3 us
  blocking collectives: 13.8 us -> 0 us
    reshape x9 -> x2, local copies, waits for them, and re-layouts: 82.4 us -> 0.1 us  [the longest x1 0.1 us: body(): slot_index = (slot_index + expert_ids % per_device).reshape(-1)]
    all_to_all x1, waiting for transfers between devices: 36.1 us -> 94.8 us  [body(): lax.all_to_all(send_part, 'expert', split_axis=0, concat_axis=0, tiled=True)]
    ppermute x2, waiting for transfers between devices: 21.8 us -> 70.4 us  [swapped(): return lax.ppermute(block, axis, route)]
    all_gather x1, waiting for transfers between devices: 37.9 us -> 0.01 us  [body(): proj_all = lax.all_gather(proj_moved, 'dp', axis=0)]
    all_to_all x1, waiting for transfers between devices: 36.4 us -> 0.01 us  [body(): lax.all_to_all(send_grad, 'expert', split_axis=0, concat_axis=0, tiled=True)]
    all_to_all x1, waiting for transfers between devices: 0.01 us -> 33.6 us  [body(): lax.all_to_all(row_grad, 'expert', split_axis=0, concat_axis=0, tiled=True)]
    all_to_all x1, waiting for transfers between devices: 25.7 us -> 0.01 us  [body(): lax.all_to_all(expert_out, 'expert', split_axis=0, concat_axis=0, tiled=T...]
    all_to_all x2 -> x0, local copies, waits for them, and re-layouts: 17.9 us -> none  [the longest x1 9.15 us: body(): lax.all_to_all(expert_out, 'expert', split_axis=0, concat_axis=0, tiled=T...]
  transfers between devices with their start and end apart: 10 -> 11, of which waited for: 7 -> 7; matrix products, arithmetic and copies ran while one was open for 49% -> 37% of each run, Pallas kernels for 0% -> 0%
where the time goes in v2:
time: 565 us; the launch traced here: 556 us
  waiting for transfers between devices  262 us (46%)
  matrix products  94.8 us (17%)
  other arithmetic  77.3 us (14%)
  local copies, waits for them, and re-layouts  68.7 us (12%)
  starting transfers between devices  38.2 us (7%)
  between operations  15.2 us (3%)
    all_to_all x1, waiting for transfers between devices, body(): lax.all_to_all(send_part, 'expert', split_axis=0, concat_axis=0, tiled=True)  94.8 us
    ppermute x2, waiting for transfers between devices, swapped(): return lax.ppermute(block, axis, route)  70.4 us
    all_to_all x1, waiting for transfers between devices, body(): lax.all_to_all(send_x, 'expert', split_axis=0, concat_axis=0, tiled=True)  45.3 us
    scatter x1, other arithmetic, body(): send_part = jnp.zeros((EXPERTS * replicas * CAP, 2 * part_width), jnp.bfl...  35.6 us
    all_to_all x1, waiting for transfers between devices, body(): lax.all_to_all(row_grad, 'expert', split_axis=0, concat_axis=0, tiled=True)  33.6 us
    dot_general x1, matrix products, body(): jnp.einsum('ncsf,sdf->ncsd', proj_grad, weight_in, preferred_element_type...  23.3 us
    dot_general x1, matrix products, body(): jnp.einsum('ncsd,sdf->ncsf', recv_x, weight_in, preferred_element_type=jn...  21.8 us
    dot_general x1, matrix products, body(): jnp.einsum('ncsd,sfd->ncsf', recv_grad, weight_down, preferred_element_ty...  17.4 us
  transfers between devices with their start and end apart: 11, of which 7 were waited for; matrix products, arithmetic and copies ran while one was open for 37% of the time, Pallas kernels for 0%

profile of v2, /device:TPU:0, one launch (start us, length us, event | category | flops | bytes accessed | tf_op | source)
XLA Modules:
  0.0 555.8 jit_solution(9920090307099460659)
XLA Ops:
  11.7 6.3 %all-to-all-start.1 = ((f32[4,128,16]{1,2,0:T(8,128)}), f32[4,128,16]{1,2,0:T(8,128)S(1)}, u32[]{:S(2)}, u32[]{:S(2)}) async-start(f32[4,128,16]{1,2,0:T(8,128)} %broadcast_in_dim.82), calls=%async_computation.1 | async-start | bytes 65536 | tf_op jit(solution)/shard_map/all_to_all | solution.py:55
  23.7 3.5 all-to-all-start
  27.4 9.7 %scatter_custom_fusion = bf16[1280,2048]{1,0:T(8,128)(2,1)} fusion(s32[1024]{0:T(1024)S(1)} %bitcast.102, bf16[]{:T(256)} %constant.79.clone.1, bf16[128,2048]{1,0:T(8,128)(2,1)S(1)} %copy-done), kind=kCustom, calls=%fused_computation.39 | custom fusion | bytes 5767170 | tf_op jit(solution)/shard_map/scatter | solution.py:67
  37.1 14.6 %all-to-all-done = bf16[2,128,2048]{1,0,2:T(2,128)(2,1)S(1)} async-done(((bf16[2,128,2048]{1,0,2:T(2,128)(2,1)}), bf16[2,128,2048]{1,0,2:T(2,128)(2,1)S(1)}, u32[]{:S(2)}, u32[]{:S(2)}) %all-to-all-start) | async-done | bytes 1048608 | tf_op jit(solution)/shard_map/all_to_all | solution.py:58
  52.5 4.8 all-to-all-start.2
  58.9 10.3 %scatter_custom_fusion.2 = bf16[1280,2048]{1,0:T(8,128)(2,1)} fusion(s32[1024]{0:T(1024)S(1)} %bitcast.103, f32[1024]{0:T(1024)S(1)} %mul.131, f32[128,2048]{1,0:T(8,128)S(1)} %convert_element_type.81, bf16[]{:T(256)} %constant.79.clone.1), kind=kCustom, calls=%fused_computation.37 | custom fusion | flops 4194304 | bytes 6295554 | tf_op jit(solution)/shard_map/scatter | solution.py:70
  72.3 45.3 %all-to-all-done.2 = bf16[8,20,8,2048]{3,2,1,0:T(8,128)(2,1)} async-done(((bf16[8,20,8,2048]{3,2,1,0:T(8,128)(2,1)}), bf16[8,20,8,2048]{3,2,1,0:T(8,128)(2,1)}, u32[]{:S(2)}, u32[]{:S(2)}) %all-to-all-start.2) | async-done | bytes 5242912 | tf_op jit(solution)/shard_map/all_to_all | solution.py:73
  117.6 4.6 all-to-all-start.4
  122.3 21.8 %fusion.52 = f32[8,20,8,768]{3,1,0,2:T(8,128)} fusion(bf16[8,2048,768]{2,1,0:T(8,128)(2,1)} %param.11, bf16[8,20,8,2048]{3,2,1,0:T(8,128)(2,1)} %all-to-all-done.2), kind=kOutput, calls=%fused_computation.57 | convolution fusion | flops 4026531840 | bytes 34340864 | tf_op jit(solution)/shard_map/ncsd,sdf->ncsf/dot_general | solution.py:91
  144.1 3.0 multiply_convert_fusion
  153.1 35.6 %scatter_custom_fusion.1 = bf16[5120,1024]{1,0:T(8,128)(2,1)} fusion(s32[4096]{0:T(1024)S(1)} %bitcast.101, bf16[4096,512]{1,0:T(8,128)(2,1)} %fusion.17, bf16[]{:T(256)} %constant.96, bf16[4096,512]{1,0:T(8,128)(2,1)} %broadcast_bitcast_fusion, bf16[]{:T(256)} %constant.79.clone.1), kind=kCustom, calls=%fused_computation.19 | custom fusion | flops 16777216 | bytes 18874372 | tf_op jit(solution)/shard_map/scatter | solution.py:87
  188.8 14.0 %collective-permute-done = bf16[8,20,8,384]{3,2,1,0:T(8,128)(2,1)} collective-permute-done((bf16[8,20,8,384]{3,2,1,0:T(8,128)(2,1)}, bf16[8,20,8,384]{3,2,1,0:T(8,128)(2,1)}, u32[]{:S(2)}, u32[]{:S(2)}) %collective-permute-start) | collective-permute-done | bytes 983072 | tf_op jit(solution)/shard_map/ppermute | solution.py:19
  202.8 4.5 copy_select_fusion.1
  207.3 8.0 %convert_bitcast_fusion.1 = bf16[8,20,8,2048]{3,1,0,2:T(8,128)(2,1)S(1)} fusion(bf16[8,20,8,384]{3,1,0,2:T(8,128)(2,1)S(1)} %multiply_convert_fusion, bf16[8,384,2048]{2,1,0:T(8,128)(2,1)} %param.12), kind=kOutput, calls=%fused_computation.33 | convolution fusion | flops 2015887360 | bytes 18808832 | tf_op jit(solution)/shard_map/ncsf,sfd->ncsd/dot_general | solution.py:102
  215.4 5.3 copy.101
  220.7 5.1 all-to-all-start.3
  225.8 17.4 %fusion.49 = (bf16[8,20,8,384]{3,1,0,2:T(8,128)(2,1)S(1)}, bf16[8,20,8,384]{3,1,0,2:T(8,128)(2,1)S(1)}) fusion(f32[8,20,8,768]{3,1,0,2:T(8,128)} %fusion.52, bf16[8,384,2048]{2,1,0:T(8,128)(2,1)} %param.12, bf16[8,20,8,2048]{3,2,1,0:T(8,128)(2,1)} %all-to-all-done.4), kind=kOutput, calls=%fused_computation.51 | convolution fusion | flops 2019655680 | bytes 23724032 | tf_op jit(solution)/shard_map/ncsd,sfd->ncsf/dot_general | solution.py:105
  247.7 23.3 %convert_bitcast_fusion = bf16[8,20,8,2048]{3,1,0,2:T(8,128)(2,1)} fusion(bf16[8,2048,768]{2,1,0:T(8,128)(2,1)} %param.11, bf16[8,20,8,384]{3,1,0,2:T(8,128)(2,1)S(1)} %get-tuple-element.51, bf16[8,20,8,384]{3,1,0,2:T(8,128)(2,1)S(1)} %get-tuple-element.50), kind=kOutput, calls=%fused_computation.32 | convolution fusion | flops 4033085440 | bytes 32374784 | tf_op jit(solution)/shard_map/ncsf,sdf->ncsd/dot_general | solution.py:111
  271.0 56.3 %collective-permute-done.1 = bf16[8,20,8,768]{3,2,1,0:T(8,128)(2,1)} collective-permute-done((bf16[8,20,8,768]{3,2,1,0:T(8,128)(2,1)}, bf16[8,20,8,768]{3,2,1,0:T(8,128)(2,1)}, u32[]{:S(2)}, u32[]{:S(2)}) %collective-permute-start.1) | collective-permute-done | bytes 1966112 | tf_op jit(solution)/shard_map/ppermute | solution.py:19
  327.4 3.7 copy_select_fusion
  331.0 5.1 all-to-all-start.6
  337.0 12.0 %gather_fusion = bf16[1024,2048]{1,0:T(8,128)(2,1)} fusion(bf16[1280,2048]{1,0:T(8,128)(2,1)} %bitcast.14, s32[1024]{0:T(1024)S(1)} %broadcast_clamp_fusion), kind=kCustom, calls=%fused_computation | custom fusion | bytes 8392704 | tf_op jit(solution)/shard_map/gather | solution.py:136
  348.9 9.0 %copy.110 = bf16[8,20,8,2048]{3,2,1,0:T(8,128)(2,1)} copy(bf16[8,20,8,2048]{3,1,0,2:T(8,128)(2,1)} %convert_bitcast_fusion) | data formatting | bytes 10485760 | tf_op jit(solution)/shard_map/optimization_barrier | solution.py:115
  357.9 94.8 %all-to-all-done.6 = bf16[8,4,20,8,1024]{4,3,2,1,0:T(8,128)(2,1)} async-done(((bf16[8,4,20,8,1024]{4,3,2,1,0:T(8,128)(2,1)}), bf16[8,4,20,8,1024]{4,3,2,1,0:T(8,128)(2,1)}, u32[]{:S(2)}, u32[]{:S(2)}) %all-to-all-start.6) | async-done | bytes 10485792 | tf_op jit(solution)/shard_map/all_to_all | solution.py:119
  452.7 4.7 all-to-all-start.5
  457.4 5.7 %fusion.11 = (f32[128,8]{1,0:T(8,128)S(1)}, bf16[128,2048]{1,0:T(8,128)(2,1)}) fusion(bf16[1024,2048]{1,0:T(8,128)(2,1)} %gather_fusion, f32[128,2048]{1,0:T(8,128)S(1)} %convert_element_type.81, f32[128,8]{1,0:T(8,128)S(1)} %copy.94), kind=kLoop, calls=%fused_computation.18 | loop fusion | flops 10222592 | bytes 5775360 | tf_op jit(solution)/shard_map/reduce_sum | solution.py:139
  463.8 9.4 %fusion.81 = (bf16[8,4,20,8,512]{4,3,2,1,0:T(8,128)(2,1)}, bf16[8,4,20,8,512]{4,3,2,1,0:T(8,128)(2,1)}) fusion(bf16[8,4,20,8,1024]{4,3,2,1,0:T(8,128)(2,1)} %all-to-all-done.6), kind=kLoop, calls=%fused_computation.118 | loop fusion | bytes 20971520 | tf_op jit(solution)/shard_map/slice | solution.py:132
  473.2 11.0 %fusion.40 = f32[8,384,512]{2,1,0:T(8,128)} fusion(bf16[8,4,20,8,512]{4,3,2,1,0:T(8,128)(2,1)} %get-tuple-element.48, bf16[4,8,20,8,384]{4,2,1,0,3:T(8,128)(2,1)} %bitcast.106), kind=kOutput, calls=%fused_computation.43 | convolution fusion | flops 2013265920 | bytes 15466496 | tf_op jit(solution)/shard_map/rncsf,nrcsd->sfd/dot_general | solution.py:129
  484.2 33.6 %all-to-all-done.5 = bf16[8,20,8,2048]{3,2,1,0:T(8,128)(2,1)} async-done(((bf16[8,20,8,2048]{3,2,1,0:T(8,128)(2,1)}), bf16[8,20,8,2048]{3,2,1,0:T(8,128)(2,1)}, u32[]{:S(2)}, u32[]{:S(2)}) %all-to-all-start.5) | async-done | bytes 5242912 | tf_op jit(solution)/shard_map/all_to_all | solution.py:120
  517.8 12.0 %gather_fusion.1 = bf16[1024,2048]{1,0:T(8,128)(2,1)} fusion(bf16[1280,2048]{1,0:T(8,128)(2,1)} %bitcast.31, s32[1024]{0:T(1024)S(1)} %broadcast_clamp_fusion), kind=kCustom, calls=%fused_computation.1 | custom fusion | bytes 8392704 | tf_op jit(solution)/shard_map/gather | solution.py:140
  529.7 5.9 %bitcast_reduce_fusion = bf16[128,2048]{1,0:T(8,128)(2,1)} fusion(bf16[1024,2048]{1,0:T(8,128)(2,1)} %gather_fusion.1), kind=kLoop, calls=%fused_computation.38 | loop fusion | flops 1835008 | bytes 4718592 | tf_op jit(solution)/shard_map/reduce_sum | solution.py:142
  535.6 13.1 %fusion.29 = f32[8,512,768]{2,1,0:T(8,128)} fusion(bf16[4,8,20,8,768]{4,2,1,0,3:T(8,128)(2,1)} %bitcast.105, bf16[8,4,20,8,512]{4,3,2,1,0:T(8,128)(2,1)} %get-tuple-element.49), kind=kOutput, calls=%fused_computation.36 | convolution fusion | flops 4026531840 | bytes 25690112 | tf_op jit(solution)/shard_map/nrcsd,rncsf->sdf/dot_general | solution.py:123
  (54 shorter events, 27.0 us)
Async XLA Ops:
  7.2 20.2 %copy-start = (bf16[128,2048]{1,0:T(8,128)(2,1)S(1)}, bf16[128,2048]{1,0:T(8,128)(2,1)}, u32[]{:S(2)}) copy-start(bf16[128,2048]{1,0:T(8,128)(2,1)} %param.7) | copy-start | bytes 1572868
  11.7 12.0 %all-to-all-start.1 = ((f32[4,128,16]{1,2,0:T(8,128)}), f32[4,128,16]{1,2,0:T(8,128)S(1)}, u32[]{:S(2)}, u32[]{:S(2)}) async-start(f32[4,128,16]{1,2,0:T(8,128)} %broadcast_in_dim.82), calls=%async_computation.1 | async-start | bytes 65536 | tf_op jit(solution)/shard_map/all_to_all | solution.py:55
  23.7 28.1 %all-to-all-start = ((bf16[2,128,2048]{1,0,2:T(2,128)(2,1)}), bf16[2,128,2048]{1,0,2:T(2,128)(2,1)S(1)}, u32[]{:S(2)}, u32[]{:S(2)}) async-start(bf16[2,128,2048]{1,0,2:T(2,128)(2,1)} %copy.96), calls=%async_computation | async-start | bytes 2097152 | tf_op jit(solution)/shard_map/all_to_all | solution.py:58
  52.4 4.8 copy-start.1
  52.4 4.9 copy-start.2
  52.4 5.1 copy-start.3
  52.5 65.2 %all-to-all-start.2 = ((bf16[8,20,8,2048]{3,2,1,0:T(8,128)(2,1)}), bf16[8,20,8,2048]{3,2,1,0:T(8,128)(2,1)}, u32[]{:S(2)}, u32[]{:S(2)}) async-start(bf16[8,20,8,2048]{3,2,1,0:T(8,128)(2,1)} %bitcast.96), calls=%async_computation.2 | async-start | bytes 10485760 | tf_op jit(solution)/shard_map/all_to_all | solution.py:73
  117.6 89.7 %all-to-all-start.4 = ((bf16[8,20,8,2048]{3,2,1,0:T(8,128)(2,1)}), bf16[8,20,8,2048]{3,2,1,0:T(8,128)(2,1)}, u32[]{:S(2)}, u32[]{:S(2)}) async-start(bf16[8,20,8,2048]{3,2,1,0:T(8,128)(2,1)} %bitcast.95), calls=%async_computation.4 | async-start | bytes 10485760 | tf_op jit(solution)/shard_map/all_to_all | solution.py:74
  122.3 208.8 %all-gather.5.cloned.1.call-start = ((), (), s32[]{:S(2)}) async-start(), calls=%async_computation.7 | async-start | bytes 5898240 | tf_op jit(solution)/shard_map/all_gather | solution.py:101
  148.7 54.1 %collective-permute-start = (bf16[8,20,8,384]{3,2,1,0:T(8,128)(2,1)}, bf16[8,20,8,384]{3,2,1,0:T(8,128)(2,1)}, u32[]{:S(2)}, u32[]{:S(2)}) collective-permute-start(bf16[8,20,8,384]{3,2,1,0:T(8,128)(2,1)} %copy.102), channel_id=1, source_target_pairs={{0,8},{8,0},{4,12},{12,4},{16,24},{24,16},{20,28},{28,20},{1,9},{9... | collective-permute-start | bytes 2949128 | tf_op jit(solution)/shard_map/ppermute | solution.py:19
  220.7 110.3 %all-to-all-start.3 = ((bf16[8,20,8,2048]{3,2,1,0:T(8,128)(2,1)}), bf16[8,20,8,2048]{3,2,1,0:T(8,128)(2,1)}, u32[]{:S(2)}, u32[]{:S(2)}) async-start(bf16[8,20,8,2048]{3,2,1,0:T(8,128)(2,1)} %copy.101), calls=%async_computation.3 | async-start | bytes 10485760 | tf_op jit(solution)/shard_map/all_to_all | solution.py:114
  245.7 81.6 %collective-permute-start.1 = (bf16[8,20,8,768]{3,2,1,0:T(8,128)(2,1)}, bf16[8,20,8,768]{3,2,1,0:T(8,128)(2,1)}, u32[]{:S(2)}, u32[]{:S(2)}) collective-permute-start(bf16[8,20,8,768]{3,2,1,0:T(8,128)(2,1)} %copy.108), channel_id=1, source_target_pairs={{0,8},{8,0},{4,12},{12,4},{16,24},{24,16},{20,28},{28,20},{1,9},{9... | collective-permute-start | bytes 5898248 | tf_op jit(solution)/shard_map/ppermute | solution.py:19
  331.0 121.7 %all-to-all-start.6 = ((bf16[8,4,20,8,1024]{4,3,2,1,0:T(8,128)(2,1)}), bf16[8,4,20,8,1024]{4,3,2,1,0:T(8,128)(2,1)}, u32[]{:S(2)}, u32[]{:S(2)}) async-start(bf16[8,4,20,8,1024]{4,3,2,1,0:T(8,128)(2,1)} %bitcast.94), calls=%async_computation.6 | async-start | bytes 20971520 | tf_op jit(solution)/shard_map/all_to_all | solution.py:119
  336.2 181.6 %all-gather.7.cloned.1.call-start = ((), (), s32[]{:S(2)}) async-start(), calls=%async_computation.8 | async-start | bytes 11796480 | tf_op jit(solution)/shard_map/all_gather | solution.py:118
  452.7 65.0 %all-to-all-start.5 = ((bf16[8,20,8,2048]{3,2,1,0:T(8,128)(2,1)}), bf16[8,20,8,2048]{3,2,1,0:T(8,128)(2,1)}, u32[]{:S(2)}, u32[]{:S(2)}) async-start(bf16[8,20,8,2048]{3,2,1,0:T(8,128)(2,1)} %copy.110), calls=%async_computation.5 | async-start | bytes 10485760 | tf_op jit(solution)/shard_map/all_to_all | solution.py:120
Sparse Core Ops, SparseCore 0:
  207.4 87.5 all-gather.4
  338.6 166.2 all-gather.6
